TPU v7x, 32 devices: a whole 2x2x4 slice. The times are simulated.
32 devices in a mesh: ctx: 8 (over y, x, core), fsdp: 4 (over z).
Axes of the slice: x: 2, y: 2, z: 4, core: 2. Of those that a mesh axis runs over, the one named last changes fastest.
Arguments:
- events: bfloat16 [2048, 4096], P('ctx'), may hold values from -6 to 6
- tile_mask: int32 [16, 2], P('ctx'), may hold values 0 or 1
- initial_state: float32 [4, 128, 128], P('fsdp'), may hold values from -96 to 96
- w_query: bfloat16 [4096, 512], P('ctx', 'fsdp'), may hold values from -0.09375 to 0.09375
- w_key: bfloat16 [4096, 512], P('ctx', 'fsdp'), may hold values from -0.09375 to 0.09375
- w_value: bfloat16 [4096, 512], P('ctx', 'fsdp'), may hold values from -0.09375 to 0.09375
- cotangent: bfloat16 [2048, 512], P('ctx', 'fsdp'), may hold values from -6 to 6
Outputs:
- attended: bfloat16 [2048, 512], P('ctx', 'fsdp')
- events_grad: bfloat16 [2048, 4096], P('ctx')
- query_grad: bfloat16 [4096, 512], P('ctx', 'fsdp')
- key_grad: bfloat16 [4096, 512], P('ctx', 'fsdp')
- value_grad: bfloat16 [4096, 512], P('ctx', 'fsdp')
Inputs may be any that keep to these rules, and one draw needn't show every extreme that they name: `tile_mask`: only entries whose column is not above the row's tile place within its block of 256 events are read.
All inputs are finite; a program needn't handle non-finite values.
Results may differ from a plain program's by a relative error of at most 0.03.
Values may be sent and summed in bfloat16 or wider, within the bound.
A program may use at most 64 MiB of HBM per device.

v0:
```python
import jax
import jax.numpy as jnp
from jax import lax
from jax.sharding import PartitionSpec as P

HDIM = 128
TILE = 128


epsilon = 1e-06


def prefix(array, axis, combine, identity, reverse):
    count, index = (lax.axis_size(axis), lax.axis_index(axis))
    everything = lax.all_gather(array.astype(jnp.bfloat16), axis)
    start = jnp.broadcast_to(jnp.asarray(identity, array.dtype), array.shape)

    def turn(k, before):
        at = count - 1 - k if reverse else k
        reached = at > index if reverse else at < index
        new = combine(before, everything[at].astype(array.dtype))
        return jnp.where(reached, new, before)

    return lax.fori_loop(0, count, turn, start)


def allowed_pairs(mask_block, tile):
    count = mask_block.shape[0]
    size = count * tile
    row_index = lax.broadcasted_iota(jnp.int32, (size, size), 0)
    col_index = lax.broadcasted_iota(jnp.int32, (size, size), 1)
    tiled = jnp.repeat(jnp.repeat(mask_block, tile, axis=0), tile, axis=1)
    return jnp.where((col_index <= row_index) & (tiled > 0), 1.0, 0.0).astype(jnp.float32)


def add_states(earlier, later):
    return earlier + later


def block_prefix(local_term, reverse):
    return prefix(local_term, "ctx", add_states, jnp.zeros_like(local_term), reverse)


def on_device(events, tile_mask, initial_state, w_query, w_key, w_value, cotangent):
    event_count, head_width = cotangent.shape
    head_count = head_width // HDIM
    stacked = jnp.stack((w_query, w_key, w_value))
    allowed = allowed_pairs(tile_mask, TILE)
    panels = lax.all_gather(stacked, "ctx", axis=1, tiled=True)
    projected = jnp.einsum("td,kdw->ktw", events, panels, preferred_element_type=jnp.float32)
    projected = projected.astype(jnp.bfloat16).reshape(3, event_count, head_count, HDIM)
    queries, key_rows, value_rows = (projected[0], projected[1], projected[2])
    local_state = jnp.einsum(
        "thd,the->hde", key_rows, value_rows, preferred_element_type=jnp.float32
    )
    carried_bf = (block_prefix(local_state, False) + initial_state).astype(jnp.bfloat16)
    scores = (
        jnp.einsum("thd,shd->hts", queries, key_rows, preferred_element_type=jnp.float32)
        * allowed[None]
    )
    mixing = scores.astype(jnp.bfloat16)
    mixture = jnp.einsum("hts,shd->thd", mixing, value_rows, preferred_element_type=jnp.float32)
    mixture = mixture + jnp.einsum(
        "thd,hde->the", queries, carried_bf, preferred_element_type=jnp.float32
    )
    inverse_rms = lax.rsqrt(jnp.mean(mixture * mixture, axis=-1, keepdims=True) + epsilon)
    attended = (mixture * inverse_rms).astype(jnp.bfloat16).reshape(event_count, head_width)
    upstream = cotangent.reshape(event_count, head_count, HDIM).astype(jnp.float32)
    mixture_grad = (
        inverse_rms * upstream
        - mixture * inverse_rms**3 * jnp.mean(upstream * mixture, axis=-1, keepdims=True)
    ).astype(jnp.bfloat16)
    score_grad = (
        jnp.einsum("the,she->hts", mixture_grad, value_rows, preferred_element_type=jnp.float32)
        * allowed[None]
    ).astype(jnp.bfloat16)
    local_grad = jnp.einsum(
        "thd,the->hde", queries, mixture_grad, preferred_element_type=jnp.float32
    )
    later_bf = block_prefix(local_grad, True).astype(jnp.bfloat16)
    query_part = jnp.einsum(
        "hts,shd->thd", score_grad, key_rows, preferred_element_type=jnp.float32
    )
    query_part = query_part + jnp.einsum(
        "the,hde->thd", mixture_grad, carried_bf, preferred_element_type=jnp.float32
    )
    key_part = jnp.einsum("hts,thd->shd", score_grad, queries, preferred_element_type=jnp.float32)
    key_part = key_part + jnp.einsum(
        "she,hde->shd", value_rows, later_bf, preferred_element_type=jnp.float32
    )
    value_part = jnp.einsum(
        "hts,the->she", mixing, mixture_grad, preferred_element_type=jnp.float32
    )
    value_part = value_part + jnp.einsum(
        "shd,hde->she", key_rows, later_bf, preferred_element_type=jnp.float32
    )
    grads = (
        jnp.stack((query_part, key_part, value_part))
        .astype(jnp.bfloat16)
        .reshape(3, event_count, head_width)
    )
    partial_grad = jnp.einsum("ktw,kdw->td", grads, panels, preferred_element_type=jnp.float32)
    events_grad = lax.psum(partial_grad.astype(jnp.bfloat16), "fsdp")
    summed = lax.psum_scatter(
        jnp.einsum("td,ktw->dkw", events, grads, preferred_element_type=jnp.float32).astype(
            jnp.bfloat16
        ),
        "ctx",
        scatter_dimension=0,
        tiled=True,
    )
    return (attended, events_grad, summed[:, 0], summed[:, 1], summed[:, 2])


def solution(mesh):
    placed = (
        P("ctx", None),
        P("ctx", None),
        P("fsdp", None, None),
        P("ctx", "fsdp"),
        P("ctx", "fsdp"),
        P("ctx", "fsdp"),
        P("ctx", "fsdp"),
    )
    return jax.shard_map(
        on_device,
        mesh=mesh,
        in_specs=placed,
        out_specs=(
            P("ctx", "fsdp"),
            P("ctx", None),
            P("ctx", "fsdp"),
            P("ctx", "fsdp"),
            P("ctx", "fsdp"),
        ),
        check_vma=False,
    )
```

profile of v0, /device:TPU:0, one launch (start us, length us, event | category | flops | bytes accessed | tf_op | source)
XLA Modules:
  0.0 218.8 jit_solution(17502069582865382712)
XLA Ops:
  7.2 1.1 copy.24
  8.4 1.0 copy.25
  9.4 1.0 copy.26
  10.4 0.8 pad_maximum_fusion
  11.3 0.7 broadcast_compare_fusion
  12.4 0.9 copy.30
  13.3 33.6 %all-gather.4.cloned.1.call-done = bf16[3,4096,128]{1,2,0:T(8,128)(2,1)} async-done(((bf16[3,512,128]{1,2,0:T(8,128)(2,1)}), bf16[3,4096,128]{1,2,0:T(8,128)(2,1)}) %all-gather.4.cloned.1.call-update) | async-done | bytes 3145744 | tf_op jit(solution)/shard_map/all_gather | solution.py:49
  46.9 2.9 %fusion.10 = bf16[3,256,128]{1,2,0:T(8,128)(2,1)S(1)} fusion(bf16[3,4096,128]{1,2,0:T(8,128)(2,1)} %all-gather.4.cloned.1.call-done, bf16[256,4096]{1,0:T(8,128)(2,1)S(1)} %copy-done), kind=kOutput, calls=%fused_computation.14 | convolution fusion | flops 805404672 | bytes 5439488 | tf_op jit(solution)/shard_map/td,kdw->ktw/dot_general | solution.py:50
  50.0 0.2 fusion.8
  50.2 9.3 %all-gather = bf16[1024,128]{1,0:T(8,128)(2,1)S(1)} all-gather(bf16[128,128]{1,0:T(8,128)(2,1)S(1)} %convolution_convert_fusion.2), channel_id=2, replica_groups=mesh['ctx'=8,'fsdp'=4] {'ctx'}, dimensions={0}, use_global_device_ids=true | all-gather | bytes 294912 | tf_op jit(solution)/shard_map/all_gather | solution.py:15
  59.5 0.3 while.30
  60.0 0.2 fusion.25
  60.8 8.4 %all-gather.1 = bf16[1024,128]{1,0:T(8,128)(2,1)S(1)} all-gather(bf16[128,128]{1,0:T(8,128)(2,1)S(1)} %convolution_convert_fusion.1), channel_id=3, replica_groups=mesh['ctx'=8,'fsdp'=4] {'ctx'}, dimensions={0}, use_global_device_ids=true | all-gather | bytes 294912 | tf_op jit(solution)/shard_map/all_gather | solution.py:15
  69.2 0.4 while.31
  70.5 2.6 %fusion.1 = bf16[4096,3,128]{0,2,1:T(8,128)(2,1)} fusion(bf16[256,4096]{1,0:T(8,128)(2,1)S(1)} %copy-done, bf16[1,256,128]{1,2,0:T(8,128)(2,1)S(1)} %fusion.17, bf16[1,256,128]{1,2,0:T(8,128)(2,1)S(1)} %fusion.18, bf16[1,256,128]{1,2,0:T(8,128)(2,1)S(1)} %fusion.19), kind=kOutput, calls=%fused_computation.5 | convolution fusion | flops 807075840 | bytes 5439488 | tf_op jit(solution)/shard_map/td,ktw->dkw/dot_general | solution.py:105
  73.2 4.5 %fusion = bf16[256,4096]{1,0:T(8,128)(2,1)} fusion(bf16[3,4096,128]{1,2,0:T(8,128)(2,1)} %all-gather.4.cloned.1.call-done, bf16[1,256,128]{1,2,0:T(8,128)(2,1)S(1)} %fusion.17, bf16[1,256,128]{1,2,0:T(8,128)(2,1)S(1)} %fusion.18, bf16[1,256,128]{1,2,0:T(8,128)(2,1)S(1)} %fusion.19), kind=kOutput, calls=%fused_computation.4 | convolution fusion | flops 806551552 | bytes 5439488 | tf_op jit(solution)/shard_map/ktw,kdw->td/dot_general | solution.py:102
  77.7 0.7 copy.34
  78.4 41.1 %reduce-scatter.2.cloned.1.call-done = bf16[512,3,128]{0,2,1:T(8,128)(2,1)} async-done(((bf16[4096,3,128]{0,2,1:T(8,128)(2,1)}), bf16[512,3,128]{0,2,1:T(8,128)(2,1)}) %reduce-scatter.2.cloned.1.call-update) | async-done | bytes 393232 | tf_op jit(solution)/shard_map/reduce_scatter | solution.py:104
  119.6 1.1 slice_bitcast_fusion
  120.6 0.8 copy.37
  121.4 0.8 copy.36
  122.2 0.8 copy.35
  122.9 86.2 %all-reduce.2.cloned.1.call-done = bf16[256,4096]{1,0:T(8,128)(2,1)} async-done(((bf16[256,4096]{1,0:T(8,128)(2,1)}), bf16[256,4096]{1,0:T(8,128)(2,1)}) %all-reduce.2.cloned.1.call-update) | async-done | bytes 2097168 | tf_op jit(solution)/shard_map/psum | solution.py:103
  209.2 3.1 %copy.58 = bf16[256,4096]{1,0:T(8,128)(2,1)} copy(bf16[256,4096]{1,0:T(8,128)(2,1)} %all-reduce.2.cloned.1.call-done) | data formatting | bytes 4194304
  (46 shorter events, 2.6 us)
Async XLA Ops:
  7.2 39.7 %copy-start = (bf16[256,4096]{1,0:T(8,128)(2,1)S(1)}, bf16[256,4096]{1,0:T(8,128)(2,1)}, u32[]{:S(2)}) copy-start(bf16[256,4096]{1,0:T(8,128)(2,1)} %param.11) | copy-start | bytes 6291460
  7.2 39.7 %all-gather.4.cloned.1.call-start = ((), (), s32[]{:S(2)}) async-start(), calls=%async_computation.1 | async-start | bytes 3538944 | tf_op jit(solution)/shard_map/all_gather | solution.py:49
  11.2 108.4 %reduce-scatter.2.cloned.1.call-start = ((), (), s32[]{:S(2)}) async-start(), calls=%async_computation.3 | async-start | bytes 3538944 | tf_op jit(solution)/shard_map/reduce_scatter | solution.py:104
  13.3 46.5 %copy-start.1 = (f32[1,128,128]{2,1,0:T(8,128)S(1)}, f32[1,128,128]{2,1,0:T(8,128)}, u32[]{:S(2)}) copy-start(f32[1,128,128]{2,1,0:T(8,128)} %param.13) | copy-start | bytes 196612
  73.1 136.0 %all-reduce.2.cloned.1.call-start = ((), (), s32[]{:S(2)}) async-start(), calls=%async_computation.2 | async-start | bytes 4194304 | tf_op jit(solution)/shard_map/psum | solution.py:103
Sparse Core Ops, SparseCore 0:
  11.3 35.5 all-gather.3
  73.3 46.2 reduce-scatter.1
  122.6 86.4 all-reduce.1
where the time goes:
time: 219 us
  waiting for transfers between devices  161 us (74%)
  blocking collectives  17.6 us (8%)
  between operations  13.9 us (6%)
  matrix products  12.2 us (6%)
  local copies, waits for them, and re-layouts  11.7 us (5%)
    psum x1, waiting for transfers between devices, on_device(): events_grad = lax.psum(partial_grad.astype(jnp.bfloat16), 'fsdp')  86.2 us
    reduce_scatter x1, waiting for transfers between devices, on_device(): lax.psum_scatter(jnp.einsum('td,ktw->dkw', events, grads, preferred_eleme...  41.1 us
    all_gather x1, waiting for transfers between devices, on_device(): panels = lax.all_gather(stacked, 'ctx', axis=1, tiled=True)  33.6 us
    all_gather x2, blocking collectives, prefix(): everything = lax.all_gather(array.astype(jnp.bfloat16), axis)  17.6 us
    unnamed x15, local copies, waits for them, and re-layouts  10.3 us
    dot_general x1, matrix products, on_device(): jnp.einsum('ktw,kdw->td', grads, panels, preferred_element_type=jnp.float32)  4.49 us
  transfers between devices with their start and end apart: 3, of which 3 were waited for; matrix products, arithmetic and copies ran while one was open for 5% of the time, Pallas kernels for 0%

commit v1 on v0

--- a/solution.py
+++ b/solution.py
@@ -1,6 +1,8 @@
 import jax
 import jax.numpy as jnp
 from jax import lax
+from jax.experimental import pallas as pl
+from jax.experimental.pallas import tpu as pltpu
 from jax.sharding import PartitionSpec as P
 
 HDIM = 128
@@ -112,7 +114,310 @@
     return (attended, events_grad, summed[:, 0], summed[:, 1], summed[:, 2])
 
 
+BF = jnp.bfloat16
+F32 = jnp.float32
+MESH = pl.DeviceIdType.MESH
+ZN = 4
+
+
+def mm(a, b, ca=1, cb=0):
+    return lax.dot_general(a, b, (((ca,), (cb,)), ((), ())), preferred_element_type=F32)
+
+
+def fused_kernel(
+    ev_hbm, mask_ref, init_ref, wq_ref, wk_ref, wv_ref, cot_ref,
+    att_ref, eg_ref, gq_ref, gk_ref, gv_ref,
+    ev, evt, panels, st1, st2, zg, acc_ref,
+    sib_out, sib_in, piece, xd, yd, xr, yr,
+    ev_sem, ag_s, ag_r, st1_s, st1_r, st2_s, st2_r, rs_s, rs_r, zw_s, zw_r, zg_s, zg_r,
+):
+    depth = wq_ref.shape[0]
+    half = depth // 2
+    me = lax.axis_index("ctx")
+    h = lax.axis_index("fsdp")
+    core = me % 2
+    xx = (me // 2) % 2
+    yy = me // 4
+    d1, d2, d4 = 1 - 2 * core, 2 - 4 * xx, 4 - 8 * yy
+    peer = [me, me + d1, me + d2, me + d1 + d2, me + d4, me + d1 + d4, me + d2 + d4, me + d1 + d2 + d4]
+    zpeer = [h, h + 1 - 2 * (h % 2), h + 2 - 4 * (h // 2), 3 - h]
+
+    def copy(src, dst, ssem, rsem, target):
+        return pltpu.make_async_remote_copy(
+            src_ref=src, dst_ref=dst, send_sem=ssem, recv_sem=rsem, device_id=target, device_id_type=MESH
+        )
+
+    ev_copy = pltpu.make_async_copy(ev_hbm, ev, ev_sem)
+    ev_copy.start()
+    barrier = pltpu.get_barrier_semaphore()
+    for r in range(1, 8):
+        pl.semaphore_signal(barrier, inc=1, device_id={"ctx": peer[r]}, device_id_type=MESH)
+    for z in range(1, ZN):
+        pl.semaphore_signal(barrier, inc=1, device_id={"fsdp": zpeer[z]}, device_id_type=MESH)
+    panels[0, :, 0:128] = wq_ref[...]
+    panels[0, :, 128:256] = wk_ref[...]
+    panels[0, :, 256:384] = wv_ref[...]
+    pl.semaphore_wait(barrier, 10)
+
+    rows = (pl.ds(0, half), pl.ds(half, half))
+
+    def gather(z, k, slot, part, to_slot, via):
+        return copy(
+            panels.at[8 * z + slot, rows[part]],
+            panels.at[8 * z + to_slot, rows[part]],
+            ag_s.at[14 * z + k],
+            ag_r.at[14 * z + k],
+            {"ctx": peer[via]},
+        )
+
+    plan = (
+        (0, 0, 2, 2), (0, 1, 2, 2), (0, 1, 4, 4), (0, 0, 4, 4), (0, 0, 1, 1), (0, 1, 1, 1), (2, 0, 6, 4), (4, 1, 6, 2),
+        (2, 0, 3, 1), (2, 1, 3, 1), (4, 0, 5, 1), (4, 1, 5, 1), (6, 0, 7, 1), (6, 1, 7, 1),
+    )
+    moves = [[gather(z, k, *plan[k]) for k in range(14)] for z in range(ZN)]
+    z_weights = [
+        copy(panels.at[0], panels.at[8 * z], zw_s.at[z], zw_r.at[z], {"fsdp": zpeer[z]}) for z in range(1, ZN)
+    ]
+    z_grads = [copy(zg.at[0], zg.at[z], zg_s.at[z], zg_r.at[z], {"fsdp": zpeer[z]}) for z in range(1, ZN)]
+
+    def send_own(z):
+        if z:
+            z_weights[z - 1].wait_recv()
+        for k in (0, 2, 1, 3, 4, 5):
+            moves[z][k].start()
+
+    def forward(z):
+        for k, onward in ((0, (6, 8)), (2, (7, 11)), (1, (9,)), (3, (10,))):
+            moves[z][k].wait_recv()
+            for other in onward:
+                moves[z][other].start()
+
+    def share(z):
+        for k, other in ((6, 12), (7, 13)):
+            moves[z][k].wait_recv()
+            moves[z][other].start()
+
+    def gathered(z):
+        for k in (4, 5, 8, 9, 10, 11, 12, 13):
+            moves[z][k].wait_recv()
+
+    send_own(0)
+    for one in z_weights:
+        one.start()
+
+    ev_copy.wait()
+    for t in range(8):
+        evt[t * depth:(t + 1) * depth, :] = ev[:, t * depth:(t + 1) * depth].T
+
+    def project(r):
+        start = pl.multiple_of(peer[r] * depth, depth)
+        return mm(ev[:, pl.ds(start, depth)], panels[r])
+
+    forward(0)
+    send_own(1)
+    acc = project(0)
+    acc += project(2)
+    acc += project(4)
+    share(0)
+    acc += project(6)
+    gathered(0)
+    for r in (1, 3, 5, 7):
+        acc += project(r)
+
+    proj = acc.astype(BF)
+    q, k, v = proj[:, 0:128], proj[:, 128:256], proj[:, 256:384]
+
+    def exchange(buf, ssem, rsem):
+        sends = [copy(buf.at[0], buf.at[r], ssem.at[r], rsem.at[r], {"ctx": peer[r]}) for r in (6, 7, 2, 4, 3, 5, 1)]
+        for one in sends:
+            one.start()
+        return sends
+
+    st1[0] = mm(k, v, 0, 0).astype(BF)
+    sends1 = exchange(st1, st1_s, st1_r)
+    f00 = jnp.where(mask_ref[0, 0] > 0, 1.0, 0.0)
+    f10 = jnp.where(mask_ref[1, 0] > 0, 1.0, 0.0)
+    f11 = jnp.where(mask_ref[1, 1] > 0, 1.0, 0.0)
+    size = 2 * TILE
+    ri = lax.broadcasted_iota(jnp.int32, (size, size), 0)
+    ci = lax.broadcasted_iota(jnp.int32, (size, size), 1)
+    factor = jnp.where(ri >= TILE, jnp.where(ci >= TILE, f11, f10), f00)
+    allowed = jnp.where(ci <= ri, factor, 0.0)
+    mixing = (mm(q, k, 1, 1) * allowed).astype(BF)
+    mixture = mm(mixing, v)
+    up = cot_ref[...].astype(F32)
+    forward(1)
+    send_own(2)
+    for one in sends1:
+        one.wait_recv()
+    carried = init_ref[0]
+    for r in range(1, 8):
+        carried += jnp.where(peer[r] < me, 1.0, 0.0) * st1[r].astype(F32)
+    carried_bf = carried.astype(BF)
+    mixture = mixture + mm(q, carried_bf)
+    inv = lax.rsqrt(jnp.mean(mixture * mixture, axis=-1, keepdims=True) + epsilon)
+    att_ref[...] = (mixture * inv).astype(BF)
+    mg = (inv * up - mixture * (inv * inv * inv) * jnp.mean(up * mixture, axis=-1, keepdims=True)).astype(BF)
+    st2[0] = mm(q, mg, 0, 0).astype(BF)
+    sends2 = exchange(st2, st2_s, st2_r)
+    share(1)
+    sgrad = (mm(mg, v, 1, 1) * allowed).astype(BF)
+    q_part = (mm(sgrad, k) + mm(mg, carried_bf, 1, 1)).astype(BF)
+    k_local = mm(sgrad, q, 0, 0)
+    v_local = mm(mixing, mg, 0, 0)
+    for one in sends2:
+        one.wait_recv()
+    later = jnp.zeros((HDIM, HDIM), F32)
+    for r in range(1, 8):
+        later += jnp.where(peer[r] > me, 1.0, 0.0) * st2[r].astype(F32)
+    later_bf = later.astype(BF)
+    k_part = (k_local + mm(v, later_bf, 1, 1)).astype(BF)
+    v_part = (v_local + mm(k, later_bf)).astype(BF)
+    grads = jnp.concatenate([q_part, k_part, v_part], axis=1)
+
+    zg[0] = grads
+    for one in z_grads:
+        one.start()
+
+    def weight_term(r):
+        start = pl.multiple_of(peer[r] * depth, depth)
+        return mm(evt[pl.ds(start, depth), :], grads)
+
+    sib = [copy(sib_out.at[i], sib_in.at[i], rs_s.at[i], rs_r.at[i], {"ctx": peer[1]}) for i in range(4)]
+    to_x = {"ctx": peer[2]}
+    to_y = {"ctx": peer[4]}
+    dx = copy(piece.at[3, rows[0]], xd, rs_s.at[4], rs_r.at[4], to_x)
+    dy = copy(piece.at[3, rows[1]], yd, rs_s.at[5], rs_r.at[5], to_y)
+    px0 = copy(piece.at[1, rows[0]], xr.at[rows[0]], rs_s.at[6], rs_r.at[6], to_x)
+    px1 = copy(piece.at[1, rows[1]], xr.at[rows[1]], rs_s.at[7], rs_r.at[7], to_x)
+    py0 = copy(piece.at[2, rows[0]], yr.at[rows[0]], rs_s.at[8], rs_r.at[8], to_y)
+    py1 = copy(piece.at[2, rows[1]], yr.at[rows[1]], rs_s.at[9], rs_r.at[9], to_y)
+
+    def rs_step0():
+        for i in (3, 1, 2, 0):
+            sib_out[i] = weight_term(2 * i + 1).astype(BF)
+            sib[i].start()
+
+    def rs_step1():
+        for i in (3, 1, 2, 0):
+            term = weight_term(2 * i)
+            sib[i].wait_recv()
+            piece[i] = (term + sib_in[i].astype(F32)).astype(BF)
+            if i == 3:
+                dx.start()
+                dy.start()
+            if i == 1:
+                px0.start()
+            if i == 2:
+                py1.start()
+
+    def rs_step2():
+        dx.wait_recv()
+        piece[2, rows[0]] = (piece[2, rows[0]].astype(F32) + xd[...].astype(F32)).astype(BF)
+        py0.start()
+        dy.wait_recv()
+        piece[1, rows[1]] = (piece[1, rows[1]].astype(F32) + yd[...].astype(F32)).astype(BF)
+        px1.start()
+
+    def rs_step3():
+        for one in (px0, py1, px1, py0):
+            one.wait_recv()
+        total = (piece[0].astype(F32) + xr[...].astype(F32) + yr[...].astype(F32)).astype(BF)
+        gq_ref[...] = total[:, 0:128]
+        gk_ref[...] = total[:, 128:256]
+        gv_ref[...] = total[:, 256:384]
+
+    def add_group(z, last=False):
+        theirs = zg[z]
+        for r in range(8):
+            term = mm(theirs, panels[8 * z + r], 1, 1)
+            if z:
+                term = acc_ref[r] + term
+            if last:
+                eg_ref[:, pl.ds(pl.multiple_of(peer[r] * depth, depth), depth)] = term.astype(BF)
+            else:
+                acc_ref[r] = term
+
+    rs_step0()
+    forward(2)
+    send_own(3)
+    rs_step1()
+    add_group(0)
+    share(2)
+    rs_step2()
+    gathered(1)
+    z_grads[0].wait_recv()
+    add_group(1)
+    forward(3)
+    share(3)
+    gathered(2)
+    z_grads[1].wait_recv()
+    add_group(2)
+    rs_step3()
+    gathered(3)
+    z_grads[2].wait_recv()
+    add_group(3, True)
+
+    for one in sum(moves, []) + z_weights + z_grads + sends1 + sends2 + sib:
+        one.wait_send()
+    for one in (dx, dy, px0, px1, py0, py1):
+        one.wait_send()
+
+
+def fused(events, tile_mask, initial_state, w_query, w_key, w_value, cotangent):
+    tokens, width = events.shape
+    depth, head = w_query.shape
+    half = depth // 2
+    wide = 3 * head
+    vm = pl.BlockSpec(memory_space=pltpu.VMEM)
+    dma = pltpu.SemaphoreType.DMA
+    return pl.pallas_call(
+        fused_kernel,
+        out_shape=(
+            jax.ShapeDtypeStruct((tokens, head), BF),
+            jax.ShapeDtypeStruct((tokens, width), BF),
+            jax.ShapeDtypeStruct((depth, head), BF),
+            jax.ShapeDtypeStruct((depth, head), BF),
+            jax.ShapeDtypeStruct((depth, head), BF),
+        ),
+        in_specs=[
+            pl.BlockSpec(memory_space=pl.ANY),
+            pl.BlockSpec(memory_space=pltpu.SMEM),
+            vm, vm, vm, vm, vm,
+        ],
+        out_specs=(vm, vm, vm, vm, vm),
+        scratch_shapes=[
+            pltpu.VMEM((tokens, width), BF),
+            pltpu.VMEM((width, tokens), BF),
+            pltpu.VMEM((8 * ZN, depth, wide), BF),
+            pltpu.VMEM((8, head, head), BF),
+            pltpu.VMEM((8, head, head), BF),
+            pltpu.VMEM((ZN, tokens, wide), BF),
+            pltpu.VMEM((8, tokens, depth), F32),
+            pltpu.VMEM((4, depth, wide), BF),
+            pltpu.VMEM((4, depth, wide), BF),
+            pltpu.VMEM((4, depth, wide), BF),
+            pltpu.VMEM((half, wide), BF),
+            pltpu.VMEM((half, wide), BF),
+            pltpu.VMEM((depth, wide), BF),
+            pltpu.VMEM((depth, wide), BF),
+            dma(()),
+            dma((14 * ZN,)), dma((14 * ZN,)),
+            dma((8,)), dma((8,)), dma((8,)), dma((8,)),
+            dma((10,)), dma((10,)),
+            dma((ZN,)), dma((ZN,)), dma((ZN,)), dma((ZN,)),
+        ],
+        compiler_params=pltpu.CompilerParams(
+            collective_id=0, has_side_effects=True, vmem_limit_bytes=56 * 1024 * 1024
+        ),
+        cost_estimate=pl.CostEstimate(
+            flops=2 * tokens * width * wide * 3, bytes_accessed=6 * tokens * width, transcendentals=tokens
+        ),
+    )(events, tile_mask, initial_state, w_query, w_key, w_value, cotangent)
+
+
 def solution(mesh):
+    on_grid = mesh.shape["ctx"] == 8 and mesh.shape["fsdp"] == 4
     placed = (
         P("ctx", None),
         P("ctx", None),
@@ -123,7 +428,7 @@
         P("ctx", "fsdp"),
     )
     return jax.shard_map(
-        on_device,
+        fused if on_grid else on_device,
         mesh=mesh,
         in_specs=placed,
         out_specs=(

time: 219 us -> 99.6 us (0.45)
  waiting for transfers between devices: 161 us -> 0 us
  Pallas kernels: 0 us -> 92.2 us
  blocking collectives: 17.6 us -> 0 us
  between operations: 13.9 us -> 0.65 us
  matrix products: 12.2 us -> 0 us
  local copies, waits for them, and re-layouts: 11.7 us -> 6.63 us
    pallas_call x0 -> x1, Pallas kernels: none -> 92.2 us  [fused(): pl.pallas_call(fused_kernel, out_shape=(jax.ShapeDtypeStruct((tokens, hea...]
    psum x1 -> x0, waiting for transfers between devices: 86.2 us -> none  [on_device(): events_grad = lax.psum(partial_grad.astype(jnp.bfloat16), 'fsdp')]
    reduce_scatter x1 -> x0, waiting for transfers between devices: 41.1 us -> none  [on_device(): lax.psum_scatter(jnp.einsum('td,ktw->dkw', events, grads, preferred_eleme...]
    all_gather x1 -> x0, waiting for transfers between devices: 33.6 us -> none  [on_device(): panels = lax.all_gather(stacked, 'ctx', axis=1, tiled=True)]
    all_gather x2 -> x0, blocking collectives: 17.6 us -> none  [prefix(): everything = lax.all_gather(array.astype(jnp.bfloat16), axis)]
    dot_general x15 -> x0, matrix products: 12.2 us -> none  [the longest x1 4.49 us: on_device(): jnp.einsum('ktw,kdw->td', grads, panels, preferred_element_type=jnp.float32)]
    unnamed x15 -> x11, local copies, waits for them, and re-layouts: 10.3 us -> 6.63 us
  transfers between devices with their start and end apart: 3 -> 0, of which waited for: 3 -> 0; matrix products, arithmetic and copies ran while one was open for 5% -> 0% of each run, Pallas kernels for 0% -> 0%
where the time goes in v1:
time: 99.6 us; the launch traced here: 99.4 us
  Pallas kernels  92.2 us (93%)
  local copies, waits for them, and re-layouts  6.63 us (7%)
    pallas_call x1, Pallas kernels, fused(): pl.pallas_call(fused_kernel, out_shape=(jax.ShapeDtypeStruct((tokens, hea...  92.2 us
    unnamed x11, local copies, waits for them, and re-layouts  6.63 us

profile of v1, /device:TPU:0, one launch (start us, length us, event | category | flops | bytes accessed | tf_op | source)
XLA Modules:
  0.0 99.4 jit_solution(14735439160392143570)
XLA Ops:
  0.6 92.2 %shard_map.110 = (bf16[256,128]{1,0:T(8,128)(2,1)}, bf16[256,4096]{1,0:T(8,128)(2,1)}, bf16[512,128]{1,0:T(8,128)(2,1)}, bf16[512,128]{1,0:T(8,128)(2,1)}, bf16[512,128]{1,0:T(8,128)(2,1)}) custom-call(bf16[256,4096]{1,0:T(8,128)(2,1)} %ev_hbm.1, s32[2,2]{1,0:T(2,128)} %mask_ref.1, f32[1,128,128]{2,1,0:T(8,128)} %init_ref.1, bf16[512,128]{1,0:T(8,128)(2,1)} %wq_ref.1, ...), custom_call_target="tpu_custom_call" | custom-call | flops 2415919104 | bytes 6291456 | tf_op jit(solution)/shard_map/pallas_call | solution.py:374
  92.8 1.5 %copy.17 = bf16[256,128]{1,0:T(8,128)(2,1)} copy(bf16[256,128]{1,0:T(8,128)(2,1)} %get-tuple-element.10) | data formatting | bytes 131072
  94.3 0.0 copy-start.2
  94.3 0.0 copy-start.1
  94.3 0.0 copy-start
  94.3 3.2 %copy.18 = bf16[256,4096]{1,0:T(8,128)(2,1)} copy(bf16[256,4096]{1,0:T(8,128)(2,1)} %get-tuple-element.11) | data formatting | bytes 4194304
  97.5 0.0 copy-done.2
  97.5 0.7 copy.19
  98.1 0.0 copy-done.1
  98.1 0.7 copy.20
  98.8 0.0 copy-done
  98.8 0.7 copy.21
Async XLA Ops:
  94.3 3.2 %copy-start.2 = (bf16[512,128]{1,0:T(8,128)(2,1)S(1)}, bf16[512,128]{1,0:T(8,128)(2,1)}, u32[]{:S(2)}) copy-start(bf16[512,128]{1,0:T(8,128)(2,1)} %get-tuple-element.12) | copy-start | bytes 393220
  94.3 3.8 %copy-start.1 = (bf16[512,128]{1,0:T(8,128)(2,1)S(1)}, bf16[512,128]{1,0:T(8,128)(2,1)}, u32[]{:S(2)}) copy-start(bf16[512,128]{1,0:T(8,128)(2,1)} %get-tuple-element.13) | copy-start | bytes 393220
  94.3 4.5 %copy-start = (bf16[512,128]{1,0:T(8,128)(2,1)S(1)}, bf16[512,128]{1,0:T(8,128)(2,1)}, u32[]{:S(2)}) copy-start(bf16[512,128]{1,0:T(8,128)(2,1)} %get-tuple-element.14) | copy-start | bytes 393220
